TPU v7x, 128 devices: a whole 4x4x4 slice. The times are simulated.
128 devices in a mesh: grp: 16 (over x, y_lo, core), dev: 8 (over y_hi, z).
Axes of the slice: x: 4, y: 4 (y_hi: 2, y_lo: 2; y = y_hi * 2 + y_lo), z: 4, core: 2. Of those that a mesh axis runs over, the one named last changes fastest.
Arguments:
- tile_patches: bfloat16 [12288, 588], P(('grp', 'dev')), may hold values from -6 to 6
- w_patch: bfloat16 [588, 1536], replicated, may hold values from -0.25 to 0.25
- w_tqkv: bfloat16 [3, 1536, 1536], P(None, None, 'dev'), may hold values from -6 to 6
- w_to: bfloat16 [1536, 1536], P('dev'), may hold values from -0.15625 to 0.15625
- w_gu: bfloat16 [2, 1536, 4096], P(None, None, 'dev'), may hold values from -0.15625 to 0.15625
- w_down: bfloat16 [4096, 1536], P('dev'), may hold values from -0.09375 to 0.09375
- tile_gain: float32 [3, 1536], replicated, may hold values from 0.1 to 1.9
- w_in: bfloat16 [1536, 768], replicated, may hold values from -0.15625 to 0.15625
- slide_tokens: bfloat16 [262144, 768], P(('grp', 'dev')), may hold values from -6 to 6
- slide_gain: float32 [768], replicated, may hold values from 0.1 to 1.9
- w_sqkv: bfloat16 [3, 768, 768], replicated, may hold values from -6 to 6
- w_so: bfloat16 [768, 768], replicated, may hold values from -1.75 to 1.75
- pattern_of_group: int32 [4], replicated, may hold values from 0 to 3, each once
- new_positions: int32 [48], replicated, may hold values from 0 to 262143, as said below
Outputs:
- tile_embed: bfloat16 [48, 768], P('grp')
- slide_out: bfloat16 [262144, 768], P(('grp', 'dev'))
Inputs may be any that keep to these rules, and one draw needn't show every extreme that they name: `pattern_of_group`: each of the four patterns is used by exactly one head group. `new_positions`: distinct positions.
All inputs are finite; a program needn't handle non-finite values.
Results may differ from a plain program's by a relative error of at most 0.025.
Values may be sent and summed in bfloat16 or wider, within the bound.
A program may use at most 256 MiB of HBM per device.

v0:
```python
import jax
import jax.numpy as jnp
from jax import lax
from jax.sharding import PartitionSpec as P

TILE_HEAD = 64
PATCHES = 256
SLIDE_HEAD = 48


def from_everyone(array, axis):
    copies = jnp.broadcast_to(array, (lax.axis_size(axis), *array.shape))
    return lax.all_to_all(copies, axis, split_axis=0, concat_axis=0, tiled=True)


def laid_out(pieces, dim):
    pieces = jnp.moveaxis(pieces, 0, dim)
    dims = pieces.shape
    return pieces.reshape(*dims[:dim], dims[dim] * dims[dim + 1], *dims[dim + 2 :])


def gather_directly(array, axis, dim):
    pieces = from_everyone(array, axis)
    return laid_out(pieces, dim)


def split_up(array, dim, count):
    before, after = (array.shape[:dim], array.shape[dim + 1 :])
    return jnp.moveaxis(array.reshape(*before, count, -1, *after), dim, 0)


def summed_on_arrival(array, axis, dim):
    pieces = split_up(array, dim, lax.axis_size(axis))
    arrived = lax.all_to_all(pieces, axis, split_axis=0, concat_axis=0, tiled=True)
    return arrived.astype(jnp.float32).sum(axis=0)


def side_by_side(arrays, axis, dim, along):
    ends, at = ([], 0)
    for a in arrays[:-1]:
        at += a.shape[along]
        ends.append(at)
    both = jnp.concatenate(arrays, axis=along)
    return tuple(jnp.split(lax.all_gather(both, axis, axis=dim, tiled=True), ends, axis=along))


def layer_norm(inputs, gain):
    inputs = inputs.astype(jnp.float32)
    center = inputs - jnp.mean(inputs, axis=-1, keepdims=True)
    spread = jnp.mean(center * center, axis=-1, keepdims=True)
    return center * lax.rsqrt(spread + 1e-06) * gain


def attend_tiles(query, keys, values, scale):
    scores = jnp.einsum("bqhd,bkhd->bhqk", query, keys, preferred_element_type=jnp.float32) * scale
    probs = jax.nn.softmax(scores, axis=-1).astype(jnp.bfloat16)
    return jnp.einsum("bhqk,bkhd->bqhd", probs, values, preferred_element_type=jnp.float32).astype(
        jnp.bfloat16
    )


def attend_segment(query, keys, values, scale):
    scores = jnp.einsum("qhd,khd->hqk", query, keys, preferred_element_type=jnp.float32) * scale
    probs = jax.nn.softmax(scores, axis=-1).astype(jnp.bfloat16)
    return jnp.einsum("hqk,khd->qhd", probs, values, preferred_element_type=jnp.float32).astype(
        jnp.bfloat16
    )


def spread_tokens(local):
    return gather_directly(local, "dev", 0)


def reduce_tokens(left, right):
    return summed_on_arrival(
        jnp.dot(left, right, preferred_element_type=jnp.float32).astype(jnp.bfloat16), "dev", 0
    )


def shards(
    tile_patches,
    w_patch,
    w_tqkv,
    w_to,
    w_gu,
    w_down,
    tile_gain,
    w_in,
    slide_tokens,
    slide_gain,
    w_sqkv,
    w_so,
    pattern_of_group,
    new_positions,
):
    devices_dev = lax.axis_size("dev")
    devices_grp = lax.axis_size("grp")
    heads_here = w_tqkv.shape[2] // TILE_HEAD
    x_zero = jnp.dot(tile_patches, w_patch, preferred_element_type=jnp.float32).astype(jnp.bfloat16)
    h_one = spread_tokens(layer_norm(x_zero, tile_gain[0]).astype(jnp.bfloat16))
    number_of_tiles = h_one.shape[0] // PATCHES
    projected = [
        jnp.dot(h_one, w_tqkv[index], preferred_element_type=jnp.float32)
        .astype(jnp.bfloat16)
        .reshape(number_of_tiles, PATCHES, heads_here, TILE_HEAD)
        for index in range(3)
    ]
    attended = attend_tiles(projected[0], projected[1], projected[2], TILE_HEAD ** (-0.5)).reshape(
        number_of_tiles * PATCHES, heads_here * TILE_HEAD
    )
    x_one = (x_zero.astype(jnp.float32) + reduce_tokens(attended, w_to)).astype(jnp.bfloat16)
    h_two = spread_tokens(layer_norm(x_one, tile_gain[1]).astype(jnp.bfloat16))
    gate = jnp.dot(h_two, w_gu[0], preferred_element_type=jnp.float32)
    upward = jnp.dot(h_two, w_gu[1], preferred_element_type=jnp.float32)
    hidden = (jax.nn.silu(gate) * upward).astype(jnp.bfloat16)
    x_two = (x_one.astype(jnp.float32) + reduce_tokens(hidden, w_down)).astype(jnp.bfloat16)
    whole_two = spread_tokens(x_two)
    pooled = jnp.mean(whole_two.astype(jnp.float32).reshape(number_of_tiles, PATCHES, -1), axis=1)
    normed = layer_norm(pooled, tile_gain[2]).astype(jnp.bfloat16)
    tile_embed = jnp.dot(normed, w_in, preferred_element_type=jnp.float32).astype(jnp.bfloat16)
    every_embed = gather_directly(tile_embed, "grp", 0)
    row_count = slide_tokens.shape[0]
    place = lax.axis_index("grp") * devices_dev + lax.axis_index("dev")
    global_rows = place * row_count + lax.iota(jnp.int32, row_count)
    matches = global_rows[:, None] == new_positions[None, :]
    inserted = jnp.dot(
        matches.astype(jnp.bfloat16), every_embed, preferred_element_type=jnp.float32
    ).astype(jnp.bfloat16)
    seq = jnp.where(jnp.any(matches, axis=1)[:, None], inserted, slide_tokens)
    h_slide = layer_norm(seq, slide_gain).astype(jnp.bfloat16)
    slide_proj = [
        jnp.dot(h_slide, w_sqkv[index], preferred_element_type=jnp.float32).astype(jnp.bfloat16)
        for index in range(3)
    ]
    dilation_rates = (1, devices_dev, devices_dev * devices_grp // 4, devices_dev * devices_grp)
    width_group = slide_proj[0].shape[1] // 4
    heads_group = width_group // SLIDE_HEAD
    columns = []
    sparse = []
    for pattern in range(4):
        ratio = dilation_rates[pattern]
        group = jnp.sum(jnp.where(pattern_of_group == pattern, lax.iota(jnp.int32, 4), 0))
        column = group * width_group
        columns.append(column)

        def pick(matrix):
            part = lax.dynamic_slice_in_dim(matrix, column, width_group, 1)
            part = part.reshape(row_count // ratio, ratio, heads_group, SLIDE_HEAD)
            return jnp.stack(
                [part[:, member % ratio, member] for member in range(heads_group)], axis=1
            )

        sparse.append([pick(matrix) for matrix in slide_proj])
    segment_keys = {
        0: (
            sparse[0][1].reshape(row_count, width_group),
            sparse[0][2].reshape(row_count, width_group),
        )
    }
    near_k, near_v = side_by_side(
        (sparse[1][1].reshape(-1, width_group), sparse[1][2].reshape(-1, width_group)), "dev", 0, 1
    )
    segment_keys[1] = (near_k, near_v)
    shipped = (2, 3)
    keys_joined = jnp.concatenate(
        [sparse[pattern][1].reshape(-1, width_group) for pattern in shipped], axis=0
    )
    values_joined = jnp.concatenate(
        [sparse[pattern][2].reshape(-1, width_group) for pattern in shipped], axis=0
    )
    total_sent = keys_joined.shape[0]
    far_k, far_v = side_by_side((keys_joined, values_joined), ("grp", "dev"), 0, 1)
    far_k = far_k.reshape(-1, total_sent, width_group)
    far_v = far_v.reshape(-1, total_sent, width_group)
    offset = 0
    for pattern in shipped:
        ratio = dilation_rates[pattern]
        count = row_count // ratio
        first = place // ratio * ratio

        def segment_rows(gathered):
            block = lax.dynamic_slice_in_dim(gathered, first, ratio, 0)
            return block[:, offset : offset + count].reshape(ratio * count, width_group)

        segment_keys[pattern] = (segment_rows(far_k), segment_rows(far_v))
        offset = offset + count
    attended_slide = jnp.zeros((row_count, slide_proj[0].shape[1]), jnp.bfloat16)
    for pattern in range(4):
        ratio = dilation_rates[pattern]
        count = row_count // ratio
        keys_here = segment_keys[pattern][0].reshape(-1, heads_group, SLIDE_HEAD)
        values_here = segment_keys[pattern][1].reshape(-1, heads_group, SLIDE_HEAD)
        outputs = attend_segment(sparse[pattern][0], keys_here, values_here, SLIDE_HEAD ** (-0.5))
        placed = jnp.zeros((count, ratio, heads_group, SLIDE_HEAD), jnp.bfloat16)
        for member in range(heads_group):
            placed = placed.at[:, member % ratio, member].set(outputs[:, member])
        attended_slide = lax.dynamic_update_slice(
            attended_slide, placed.reshape(row_count, width_group), (jnp.int32(0), columns[pattern])
        )
    slide_out = (
        seq.astype(jnp.float32) + jnp.dot(attended_slide, w_so, preferred_element_type=jnp.float32)
    ).astype(jnp.bfloat16)
    return (tile_embed, slide_out)


def solution(mesh):
    placed = (
        P(("grp", "dev"), None),
        P(),
        P(None, None, "dev"),
        P("dev", None),
        P(None, None, "dev"),
        P("dev", None),
        P(),
        P(),
        P(("grp", "dev"), None),
        P(),
        P(),
        P(),
        P(),
        P(),
    )
    return jax.shard_map(
        shards,
        mesh=mesh,
        in_specs=placed,
        out_specs=(P("grp", None), P(("grp", "dev"), None)),
        check_vma=False,
    )
```

profile of v0, /device:TPU:1, one launch (start us, length us, event | category | flops | bytes accessed | tf_op | source)
XLA Modules:
  0.0 694.2 jit_solution(17670250594109128226)
XLA Ops:
  10.2 38.0 %all_to_all.30 = bf16[8,96,1536]{2,1,0:T(8,128)(2,1)S(1)} all-to-all(bf16[8,96,1536]{2,1,0:T(8,128)(2,1)S(1)} %broadcast_in_dim.19), channel_id=1, replica_groups=mesh['grp'=16,'dev'=8] {'dev'}, dimensions={0} | all-to-all | bytes 4718592 | tf_op jit(solution)/shard_map/all_to_all | solution.py:13
  63.8 31.3 %all_to_all.31 = bf16[8,96,1536]{2,1,0:T(8,128)(2,1)S(1)} all-to-all(bf16[8,96,1536]{2,1,0:T(8,128)(2,1)S(1)} %bitcast.248), channel_id=1, replica_groups=mesh['grp'=16,'dev'=8] {'dev'}, dimensions={0} | all-to-all | bytes 4718592 | tf_op jit(solution)/shard_map/all_to_all | solution.py:34
  96.3 30.3 %all_to_all.32 = bf16[8,96,1536]{2,1,0:T(8,128)(2,1)S(1)} all-to-all(bf16[8,96,1536]{2,1,0:T(8,128)(2,1)S(1)} %broadcast_in_dim.20), channel_id=1, replica_groups=mesh['grp'=16,'dev'=8] {'dev'}, dimensions={0} | all-to-all | bytes 4718592 | tf_op jit(solution)/shard_map/all_to_all | solution.py:13
  130.6 7.1 %convolution_convert_fusion.4 = bf16[768,1536]{1,0:T(8,128)(2,1)} fusion(bf16[512,1536]{1,0:T(8,128)(2,1)} %param.51, f32[768,512]{1,0:T(8,128)} %fusion.38, bf16[768,1536]{1,0:T(8,128)(2,1)} %bitcast.262, bf16[2,1536,512]{2,1,0:T(8,128)(2,1)} %param.50), kind=kOutput, calls=%fused_computation.34 | convolution fusion | flops 2419458048 | bytes 9437184 | tf_op jit(solution)/shard_map/dot_general | solution.py:76
  137.7 29.5 %all_to_all.33 = bf16[8,96,1536]{2,1,0:T(8,128)(2,1)S(1)} all-to-all(bf16[8,96,1536]{2,1,0:T(8,128)(2,1)} %bitcast.263), channel_id=1, replica_groups=mesh['grp'=16,'dev'=8] {'dev'}, dimensions={0} | all-to-all | bytes 4718592 | tf_op jit(solution)/shard_map/all_to_all | solution.py:34
  169.2 4.5 all-to-all-start.4
  176.9 4.6 copy.374
  181.6 14.8 %all-to-all-done.4 = bf16[8,96,1536]{2,1,0:T(8,128)(2,1)} async-done(((bf16[8,96,1536]{2,1,0:T(8,128)(2,1)}), bf16[8,96,1536]{2,1,0:T(8,128)(2,1)}, u32[]{:S(2)}, u32[]{:S(2)}) %all-to-all-start.4) | async-done | bytes 2359328 | tf_op jit(solution)/shard_map/all_to_all | solution.py:13
  199.8 11.9 %all-to-all-start.5 = ((bf16[16,3,768]{2,1,0:T(4,128)(2,1)}), bf16[16,3,768]{2,1,0:T(4,128)(2,1)S(1)}, u32[]{:S(2)}, u32[]{:S(2)}) async-start(bf16[16,3,768]{2,1,0:T(4,128)(2,1)} %broadcast_in_dim.26), calls=%async_computation.5 | async-start | bytes 196608 | tf_op jit(solution)/shard_map/all_to_all | solution.py:13
  212.2 5.5 all-to-all-done.5
  239.9 5.3 dynamic-slice_bitcast_fusion
  280.2 28.8 %fusion.158 = (f32[4,2048]{1,0:T(4,128)S(1)}, f32[4,2048,2048]{1,2,0:T(8,128)}) fusion(bf16[2048,1,48]{0,2,1:T(8,128)(2,1)S(1)} %get-tuple-element.280, bf16[2048,1,48]{0,2,1:T(8,128)(2,1)S(1)} %get-tuple-element.281, bf16[2048,1,48]{0,2,1:T(8,128)(2,1)S(1)} %get-tuple-element.282, bf16[2048,1,48]{0,2,1:T(8,128)(2,1)S(1)} %get-tuple-element.279, ...), kind=kOutput, calls=%fused_computation.260 | convolution fusion | flops 1663305728 | bytes 68714496 | tf_op jit(solution)/shard_map/sub | solution.py:64
  309.0 22.2 %fusion.27 = bf16[2048,4,48]{0,2,1:T(8,128)(2,1)S(1)} fusion(f32[4,2048,2048]{1,2,0:T(8,128)} %get-tuple-element.290, f32[4,2048]{1,0:T(4,128)S(1)} %get-tuple-element.289, bf16[2048,1,48]{0,2,1:T(8,128)(2,1)S(1)} %get-tuple-element.272, bf16[2048,1,48]{0,2,1:T(8,128)(2,1)S(1)} %get-tuple-element.273, bf16[2048,1,48]{0,2,1:T(8,128)(2,1)S(1)} %get-tuple-element.274, ...), kind=kOutput, calls=%fused_computation.42 | convolution fusion | flops 1645740032 | bytes 68714496 | tf_op jit(solution)/shard_map/hqk,khd->qhd/dot_general | solution.py:65
  337.1 11.4 %dynamic_update_slice.12 = bf16[2048,768]{1,0:T(8,128)(2,1)} dynamic-update-slice(bf16[2048,768]{1,0:T(8,128)(2,1)} %broadcast_in_dim.27, bf16[2048,192]{1,0:T(8,128)(2,1)S(1)} %copy.376, s32[]{:T(128)} %constant.485.clone.1, s32[]{:T(128)S(6)} %select_n.55) | dynamic-update-slice | bytes 1572868 | tf_op jit(solution)/shard_map/dynamic_update_slice | solution.py:197
  350.1 4.9 fusion.159
  354.9 4.8 fusion.53
  363.0 10.3 %dynamic_update_slice.13 = bf16[2048,768]{1,0:T(8,128)(2,1)} dynamic-update-slice(bf16[2048,768]{1,0:T(8,128)(2,1)} %dynamic_update_slice.12, bf16[2048,192]{1,0:T(8,128)(2,1)S(1)} %reshape.807, s32[]{:T(128)} %constant.485.clone.1, s32[]{:T(128)S(6)} %select_n.57) | dynamic-update-slice | bytes 1572868 | tf_op jit(solution)/shard_map/dynamic_update_slice | solution.py:197
  373.3 237.1 %all-gather.5.cloned.1.call-done = bf16[10240,384]{1,0:T(8,128)(2,1)} async-done(((bf16[80,384]{1,0:T(8,128)(2,1)}), bf16[10240,384]{1,0:T(8,128)(2,1)}) %all-gather.5.cloned.1.call-update) | async-done | bytes 7864336 | tf_op jit(solution)/shard_map/all_gather | solution.py:44
  610.5 6.0 fusion.145
  648.1 4.4 copy.421
  653.7 10.0 %dynamic_update_slice.14 = bf16[2048,768]{1,0:T(8,128)(2,1)} dynamic-update-slice(bf16[2048,768]{1,0:T(8,128)(2,1)} %dynamic_update_slice.13, bf16[2048,192]{1,0:T(8,128)(2,1)S(1)} %reshape.823, s32[]{:T(128)} %constant.485.clone.1, s32[]{:T(128)S(6)} %select_n.59) | dynamic-update-slice | bytes 1572868 | tf_op jit(solution)/shard_map/dynamic_update_slice | solution.py:197
  663.7 10.9 %dynamic_update_slice.15 = bf16[2048,768]{1,0:T(8,128)(2,1)} dynamic-update-slice(bf16[2048,768]{1,0:T(8,128)(2,1)} %dynamic_update_slice.14, bf16[2048,192]{1,0:T(8,128)(2,1)S(1)} %copy-done.3, s32[]{:T(128)} %constant.485.clone.1, s32[]{:T(128)S(6)} %select_n.61) | dynamic-update-slice | bytes 1572868 | tf_op jit(solution)/shard_map/dynamic_update_slice | solution.py:197
  674.6 7.7 %fusion.20 = bf16[2048,768]{0,1:T(8,128)(2,1)} fusion(bf16[2048,768]{0,1:T(8,128)(2,1)} %copy-done.4, bf16[2048,768]{1,0:T(8,128)(2,1)} %dynamic_update_slice.15, bf16[768,768]{1,0:T(8,128)(2,1)} %param.57), kind=kOutput, calls=%fused_computation.24 | convolution fusion | flops 2420637696 | bytes 10616832 | tf_op jit(solution)/shard_map/dot_general | solution.py:201
  682.3 4.6 copy.431
  (231 shorter events, 130.4 us)
Async XLA Ops:
  7.2 191.6 %copy-start = (bf16[1536,768]{1,0:T(8,128)(2,1)S(1)}, bf16[1536,768]{1,0:T(8,128)(2,1)}, u32[]{:S(2)}) copy-start(bf16[1536,768]{1,0:T(8,128)(2,1)} %param.53) | copy-start | bytes 7077892
  7.2 2.5 copy-start.19
  10.1 38.1 %copy-start.25 = (bf16[3,1536,192]{1,2,0:T(8,128)(2,1)S(1)}, bf16[3,1536,192]{1,2,0:T(8,128)(2,1)}, u32[]{:S(2)}) copy-start(bf16[3,1536,192]{1,2,0:T(8,128)(2,1)} %param.48) | copy-start | bytes 5308420
  60.6 2.4 copy-start.17
  96.3 31.8 %copy-start.24 = (bf16[2,1536,512]{2,1,0:T(8,128)(2,1)S(1)}, bf16[2,1536,512]{2,1,0:T(8,128)(2,1)}, u32[]{:S(2)}) copy-start(bf16[2,1536,512]{2,1,0:T(8,128)(2,1)} %param.50) | copy-start | bytes 9437188
  169.2 4.5 copy-start.20
  169.2 27.2 %all-to-all-start.4 = ((bf16[8,96,1536]{2,1,0:T(8,128)(2,1)}), bf16[8,96,1536]{2,1,0:T(8,128)(2,1)}, u32[]{:S(2)}, u32[]{:S(2)}) async-start(bf16[8,96,1536]{2,1,0:T(8,128)(2,1)} %broadcast_in_dim.21), calls=%async_computation.4 | async-start | bytes 4718592 | tf_op jit(solution)/shard_map/all_to_all | solution.py:13
  196.3 15.7 %copy-start.22 = (s32[48]{0:T(128)S(1)}, s32[48]{0:T(128)}, u32[]{:S(2)}) copy-start(s32[48]{0:T(128)} %param.59) | copy-start | bytes 580
  199.2 21.7 %copy-start.18 = (bf16[3,768]{1,0:T(4,128)(2,1)}, bf16[3,768]{1,0:T(4,128)(2,1)S(1)}, u32[]{:S(2)}) copy-start(bf16[3,768]{1,0:T(4,128)(2,1)S(1)} %convolution_convert_fusion.12) | copy-start | bytes 13828
  199.8 17.8 %all-to-all-start.5 = ((bf16[16,3,768]{2,1,0:T(4,128)(2,1)}), bf16[16,3,768]{2,1,0:T(4,128)(2,1)S(1)}, u32[]{:S(2)}, u32[]{:S(2)}) async-start(bf16[16,3,768]{2,1,0:T(4,128)(2,1)} %broadcast_in_dim.26), calls=%async_computation.5 | async-start | bytes 196608 | tf_op jit(solution)/shard_map/all_to_all | solution.py:13
  211.7 136.8 %all-gather.3.cloned.1.call-start = ((), (), s32[]{:S(2)}) async-start(), calls=%async_computation.6 | async-start | bytes 1769472 | tf_op jit(solution)/shard_map/all_gather | solution.py:44
  217.7 4.0 copy-start.23
  220.9 8.5 %copy-start.4 = (bf16[2048,768]{0,1:T(8,128)(2,1)}, bf16[2048,768]{0,1:T(8,128)(2,1)S(1)}, u32[]{:S(2)}) copy-start(bf16[2048,768]{0,1:T(8,128)(2,1)S(1)} %get-tuple-element.288) | copy-start | bytes 9437188
  245.7 7.4 %copy-start.21 = (s32[4]{0:T(128)S(1)}, s32[4]{0:T(128)}, u32[]{:S(2)}) copy-start(s32[4]{0:T(128)} %constant.491.clone.1) | copy-start | bytes 52
  250.7 359.7 %all-gather.5.cloned.1.call-start = ((), (), s32[]{:S(2)}) async-start(), calls=%async_computation.7 | async-start | bytes 7925760 | tf_op jit(solution)/shard_map/all_gather | solution.py:44
  253.9 4.1 copy-start.6
  256.5 3.0 copy-start.8
  259.5 4.1 copy-start.12
  263.6 2.4 copy-start.11
  275.6 4.4 copy-start.10
  277.7 2.4 copy-start.9
  634.1 3.8 copy-start.2
  653.7 10.0 %copy-start.3 = (bf16[2048,192]{1,0:T(8,128)(2,1)S(1)}, bf16[2048,192]{1,0:T(8,128)(2,1)}, u32[]{:S(2)}) copy-start(bf16[2048,192]{1,0:T(8,128)(2,1)} %copy.429) | copy-start | bytes 2359300
  674.6 12.3 %copy-start.1 = (bf16[1536,768]{1,0:T(8,128)(2,1)S(1)}, bf16[1536,768]{1,0:T(8,128)(2,1)}, u32[]{:S(2)}) copy-start(bf16[1536,768]{1,0:T(8,128)(2,1)} %param.53) | copy-start | bytes 7077892
  (7 other events, 11.0 us)
Sparse Core Ops, SparseCore 0:
  250.8 47.1 all-gather.2
  299.7 310.6 all-gather.4
where the time goes:
time: 704 us; the launch traced here: 694 us
  waiting for transfers between devices  257 us (37%)
  local copies, waits for them, and re-layouts  148 us (21%)
  blocking collectives  129 us (18%)
  matrix products  112 us (16%)
  between operations  18 us (3%)
  starting transfers between devices  17.1 us (2%)
  other arithmetic  12.5 us (2%)
    all_gather x2, waiting for transfers between devices, side_by_side(): lax.all_gather(both, axis, axis=dim, tiled=True)  237 us
    all_to_all x2, blocking collectives, from_everyone(): return lax.all_to_all(copies, axis, split_axis=0, concat_axis=0, tiled=True)  68.4 us
    all_to_all x2, blocking collectives, summed_on_arrival(): lax.all_to_all(pieces, axis, split_axis=0, concat_axis=0, tiled=True)  60.7 us
    dynamic_update_slice x4, local copies, waits for them, and re-layouts, shards(): lax.dynamic_update_slice(attended_slide, placed.reshape(row_count, width_...  42.6 us
    sub x3, matrix products, attend_segment(): probs = jax.nn.softmax(scores, axis=-1).astype(jnp.bfloat16)  35.8 us
    dot_general x4, matrix products, attend_segment(): jnp.einsum('hqk,khd->qhd', probs, values, preferred_element_type=jnp.floa...  31.2 us
    unnamed x74, local copies, waits for them, and re-layouts  20.5 us
    all_to_all x2, waiting for transfers between devices, from_everyone(): return lax.all_to_all(copies, axis, split_axis=0, concat_axis=0, tiled=True)  20.3 us
  transfers between devices with their start and end apart: 4, of which 3 were waited for; matrix products, arithmetic and copies ran while one was open for 18% of the time, Pallas kernels for 0%

commit v1 on v0

v1 whole, which is shorter than its diff:
```python
import functools

import jax
import jax.numpy as jnp
from jax import lax
from jax.experimental import pallas as pl
from jax.experimental.pallas import tpu as pltpu
from jax.sharding import PartitionSpec as P

MESH = pl.DeviceIdType.MESH
BF16 = jnp.bfloat16
F32 = jnp.float32

TW = 1536
TH = 64
TP = 256
HB = 192
FB = 512
SW = 768
GW = 192
SH = 48
ROWS = 2048
DIL = (1, 8, 32, 128)
LOG2E = 1.4426950408889634


def dot(a, b):
    return jnp.dot(a, b, preferred_element_type=F32)


def dot_nt(a, b):
    return lax.dot_general(a, b, (((1,), (1,)), ((), ())), preferred_element_type=F32)


def norm(v, gain):
    center = v - jnp.mean(v, axis=-1, keepdims=True)
    spread = jnp.mean(center * center, axis=-1, keepdims=True)
    return center * lax.rsqrt(spread + 1e-06) * gain


def head_of(shape):
    return (lax.broadcasted_iota(jnp.int32, shape, 1) % GW) // SH


def encoder_kernel(
    patches,
    w_patch,
    w_tqkv,
    w_to,
    w_gu,
    w_down,
    w_in,
    tokens,
    w_slide,
    tgain,
    sgain,
    qkv0_out,
    q1_out,
    q2_out,
    q3_out,
    kv1,
    kv2,
    kv3,
    em,
    new_out,
    patches_s,
    w_patch_s,
    w_tqkv_s,
    wto_s,
    w_gu_s,
    w_down_s,
    w_in_s,
    tok_s,
    w_slide_s,
    hs,
    qkv0_s,
    kvc1,
    kvc2,
    kvc3,
    x0_s,
    att_s,
    pp_s,
    load_sem,
    out_sem,
    own_sem,
    send_sem,
    recv_sem,
    att_send,
    att_recv,
):
    grp = lax.axis_index("grp")
    dev = lax.axis_index("dev")
    core = grp % 2
    plane = grp // 4
    chip = (grp // 2) * 8 + dev
    local16 = (grp // 2) % 2 * 8 + dev
    sibling = (grp // 2) * 2 + (1 - core)

    def peer8(i):
        return (grp, (dev + i) % 8)

    def peer16(i):
        to = (local16 + i) % 16
        return (plane * 4 + (to // 8) * 2 + core, to % 8)

    def peer64(i):
        to = (chip + i) % 64
        return ((to // 8) * 2 + core, to % 8)

    def cross(i):
        return (i * 2 + (1 - core), dev)

    def peer_grp(i):
        return ((grp + i) % 16, dev)

    def load(src, dst, at):
        copy = pltpu.make_async_copy(src, dst, load_sem.at[at])
        copy.start()
        return copy

    ld_tok = load(tokens, tok_s, 0)
    ld_slide = load(w_slide, w_slide_s, 1)
    ld_patch = load(w_patch, w_patch_s, 2)
    ld_tqkv = load(w_tqkv, w_tqkv_s, 3)
    ld_gu = load(w_gu, w_gu_s, 4)
    ld_down = load(w_down, w_down_s, 5)
    ld_in = load(w_in, w_in_s, 6)

    my_patch = pl.ds(pl.multiple_of(dev * 96, 32), 96)
    half_row = pl.multiple_of(core * 96, 32)
    my_half = pl.ds(pl.multiple_of(dev * HB + core * 96, 32), 96)
    my_shard = pl.ds(pl.multiple_of(dev * HB, 64), HB)

    barrier = pltpu.get_barrier_semaphore()

    @pl.loop(1, 64)
    def _(i):
        pl.semaphore_signal(barrier, inc=1, device_id=peer64(i), device_id_type=MESH)

    @pl.loop(0, 8)
    def _(i):
        pl.semaphore_signal(barrier, inc=1, device_id=cross(i), device_id_type=MESH)

    pl.semaphore_wait(barrier, 71)

    own_patch = pltpu.make_async_copy(patches, patches_s.at[my_patch], own_sem.at[0])
    own_patch.start()
    own_wto = pltpu.make_async_copy(w_to, wto_s.at[my_shard], own_sem.at[1])
    own_wto.start()

    def push(src, dst, at, to):
        pltpu.make_async_remote_copy(
            src_ref=src,
            dst_ref=dst,
            send_sem=send_sem.at[at],
            recv_sem=recv_sem.at[at],
            device_id=to,
            device_id_type=MESH,
        ).start()

    def landed(ref, sem):
        pltpu.make_async_copy(ref, ref, sem).wait()

    @pl.loop(1, 8)
    def _(i):
        push(patches, patches_s.at[my_patch], 0, peer8(i))

    @pl.loop(1, 8)
    def _(i):
        push(w_to.at[pl.ds(half_row, 96)], wto_s.at[my_half], 1, peer8(i))

    ld_tok.wait()
    ld_slide.wait()

    @pl.loop(0, 8)
    def _(c):
        at = pl.ds(pl.multiple_of(c * 256, 256), 256)
        h = norm(tok_s[at, :].astype(F32), sgain[...])
        for b in range(6):
            hs[b, at, :] = h[:, b * 128 : (b + 1) * 128]
        y = dot(h.astype(BF16), w_slide_s[0])
        ones = lax.broadcasted_iota(jnp.int32, y.shape, 1) == 2 * 256 + GW
        qkv0_s[at, :] = jnp.where(ones, 1.0, y).astype(BF16)

    out0 = pltpu.make_async_copy(qkv0_s, qkv0_out, out_sem.at[0])
    out0.start()

    own_patch.wait()
    landed(patches_s.at[pl.ds(0, 672)], recv_sem.at[0])
    ld_patch.wait()
    ld_tqkv.wait()

    lanes = lax.broadcasted_iota(jnp.int32, (TP, HB), 1) // TH

    @pl.loop(0, 3)
    def _(t):
        at = pl.ds(pl.multiple_of(t * TP, TP), TP)
        x0 = dot(patches_s[at, :], w_patch_s[...]).astype(BF16)
        x0_s[at, :] = x0
        h1 = norm(x0.astype(F32), tgain[0:1, :]).astype(BF16)
        q = dot(h1, w_tqkv_s[0]).astype(BF16)
        k = dot(h1, w_tqkv_s[1]).astype(BF16)
        vt = dot(h1, w_tqkv_s[2]).T.astype(BF16)
        for h in range(3):
            s = dot_nt(jnp.where(lanes == h, q, jnp.zeros_like(q)), k) * (TH**-0.5)
            e = jnp.exp(s - jnp.max(s, axis=-1, keepdims=True))
            probs = (e / jnp.sum(e, axis=-1, keepdims=True)).astype(BF16)
            o = dot_nt(vt[h * TH : (h + 1) * TH, :], probs)
            rows = pl.ds(pl.multiple_of(dev * HB + h * TH, 64), TH)
            att_s[t, rows, :] = o.astype(BF16)

        @pl.loop(1, 8)
        def _(i):
            pltpu.make_async_remote_copy(
                src_ref=att_s.at[t, my_shard],
                dst_ref=att_s.at[t, my_shard],
                send_sem=att_send.at[t],
                recv_sem=att_recv.at[t],
                device_id=peer8(i),
                device_id_type=MESH,
            ).start()

    for p, kvc, q_out in ((1, kvc1, q1_out), (2, kvc2, q2_out), (3, kvc3, q3_out)):
        r = DIL[p]
        n = ROWS // r
        picked = jnp.concatenate(
            [
                jnp.concatenate([hs[b, pl.ds(j, n, stride=r), :] for b in range(6)], axis=1)
                for j in range(4)
            ],
            axis=0,
        ).astype(BF16)
        y = dot(picked, w_slide_s[p])
        head = head_of((n, SW))
        mine = jnp.zeros((n, SW), F32)
        for j in range(4):
            mine = jnp.where(head == j, y[j * n : (j + 1) * n, :], mine)
        kvc[...] = mine[:, :384].astype(BF16)
        q_out[...] = mine[:, 384:].astype(BF16)

    at1 = pl.ds(pl.multiple_of(dev * 256, 256), 256)
    at2 = pl.ds(pl.multiple_of((core * 16 + local16) * 64, 64), 64)
    at3 = pl.ds(pl.multiple_of((core * 64 + chip) * 16, 16), 16)
    own1 = pltpu.make_async_copy(kvc1, kv1.at[at1], own_sem.at[2])
    own2 = pltpu.make_async_copy(kvc2, kv2.at[at2], own_sem.at[3])
    own3 = pltpu.make_async_copy(kvc3, kv3.at[at3], own_sem.at[4])
    own1.start()
    own2.start()
    own3.start()

    @pl.loop(1, 64)
    def _(i):
        push(kvc3, kv3.at[at3], 2, peer64(i))

    @pl.loop(1, 16)
    def _(i):
        push(kvc2, kv2.at[at2], 3, peer16(i))

    @pl.loop(1, 8)
    def _(i):
        push(kvc1, kv1.at[at1], 4, peer8(i))

    own_wto.wait()
    landed(wto_s.at[pl.ds(0, 672)], recv_sem.at[1])

    @pl.loop(1, 8)
    def _(i):
        half = pl.ds(pl.multiple_of(((dev + i) % 8) * HB + core * 96, 32), 96)
        push(wto_s.at[half], wto_s.at[half], 5, (sibling, dev))

    landed(wto_s.at[pl.ds(0, 672)], recv_sem.at[5])
    ld_gu.wait()

    eight = lax.broadcasted_iota(jnp.int32, (8, 1), 0)

    def feed(t, sums):
        x_sum, h_sum = sums
        at = pl.ds(pl.multiple_of(t * TP, TP), TP)
        landed(att_s.at[t, pl.ds(0, 7 * HB)], att_recv.at[t])
        att = att_s[t].T
        x1 = (x0_s[at, :].astype(F32) + dot(att, wto_s[...])).astype(BF16).astype(F32)
        h2 = norm(x1, tgain[1:2, :]).astype(BF16)
        gate = dot(h2, w_gu_s[0])
        up = dot(h2, w_gu_s[1])
        hidden = (jax.nn.silu(gate) * up).astype(BF16).astype(F32)
        x_sum = x_sum + jnp.where(eight == t, jnp.sum(x1, axis=0, keepdims=True), 0.0)
        h_sum = h_sum + jnp.where(eight == t, jnp.sum(hidden, axis=0, keepdims=True), 0.0)
        return x_sum, h_sum

    x_sum, h_sum = lax.fori_loop(
        0, 3, feed, (jnp.zeros((8, TW), F32), jnp.zeros((8, FB), F32))
    )
    ld_down.wait()
    h_mean = h_sum * (1.0 / TP)
    coarse = h_mean.astype(BF16)
    fine = (h_mean - coarse.astype(F32)).astype(BF16)
    both = jnp.concatenate([coarse.astype(F32), fine.astype(F32)], axis=0).astype(BF16)
    part = dot(both, w_down_s[...])
    pp_s[dev] = part[0:8] + part[8:16]

    @pl.loop(1, 8)
    def _(i):
        push(pp_s.at[dev], pp_s.at[dev], 6, peer8(i))

    ld_in.wait()
    landed(pp_s.at[pl.ds(0, 7)], recv_sem.at[6])
    pooled = x_sum * (1.0 / TP) + jnp.sum(pp_s[...], axis=0)
    normed = norm(pooled, tgain[2:3, :]).astype(BF16)
    em[grp] = dot(normed, w_in_s[...]).astype(BF16).astype(F32)

    @pl.loop(1, 16)
    def _(i):
        push(em.at[grp], em.at[grp], 7, peer_grp(i))

    own3.wait()
    half3 = pl.ds(pl.multiple_of(core * 1024, 1024), 1024)
    landed(kv3.at[pl.ds(0, 63 * 16)], recv_sem.at[2])
    push(kv3.at[half3], kv3.at[half3], 8, (sibling, dev))
    own2.wait()
    landed(kv2.at[pl.ds(0, 15 * 64)], recv_sem.at[3])
    push(kv2.at[half3], kv2.at[half3], 9, (sibling, dev))

    landed(em.at[pl.ds(0, 15)], recv_sem.at[7])
    fresh = norm(em[...].reshape(128, SW), sgain[...]).astype(BF16)
    for p in range(4):
        new_out[:, p * SW : (p + 1) * SW] = dot(fresh, w_slide_s[p])

    own1.wait()
    landed(kv1.at[pl.ds(0, 7 * 256)], recv_sem.at[4])
    landed(kv3.at[half3], recv_sem.at[8])
    landed(kv2.at[half3], recv_sem.at[9])
    out0.wait()

    landed(patches_s.at[pl.ds(0, 672)], send_sem.at[0])
    landed(wto_s.at[pl.ds(0, 672)], send_sem.at[1])
    landed(kv3.at[pl.ds(0, 63 * 16)], send_sem.at[2])
    landed(kv2.at[pl.ds(0, 15 * 64)], send_sem.at[3])
    landed(kv1.at[pl.ds(0, 7 * 256)], send_sem.at[4])
    landed(wto_s.at[pl.ds(0, 672)], send_sem.at[5])
    landed(pp_s.at[pl.ds(0, 7)], send_sem.at[6])
    landed(em.at[pl.ds(0, 15)], send_sem.at[7])
    landed(kv3.at[half3], send_sem.at[8])
    landed(kv2.at[half3], send_sem.at[9])

    @pl.loop(0, 3)
    def _(t):
        landed(att_s.at[t, pl.ds(0, 7 * HB)], att_send.at[t])


def run_encoder(
    patches, w_patch, w_tqkv, w_to, w_gu, w_down, w_in, tokens, w_slide, tgain, sgain
):
    hbm = pl.BlockSpec(memory_space=pl.ANY)
    vmem = pl.BlockSpec(memory_space=pltpu.VMEM)
    shape = jax.ShapeDtypeStruct
    return pl.pallas_call(
        encoder_kernel,
        out_shape=(
            shape((ROWS, SW), BF16),
            shape((256, 384), BF16),
            shape((64, 384), BF16),
            shape((16, 384), BF16),
            shape((2048, 384), BF16),
            shape((2048, 384), BF16),
            shape((2048, 384), BF16),
            shape((16, 8, SW), F32),
            shape((128, 4 * SW), F32),
        ),
        in_specs=[hbm] * 9 + [vmem] * 2,
        out_specs=(hbm, vmem, vmem, vmem, hbm, hbm, hbm, vmem, vmem),
        scratch_shapes=[
            pltpu.VMEM((768, 588), BF16),
            pltpu.VMEM((588, TW), BF16),
            pltpu.VMEM((3, TW, HB), BF16),
            pltpu.VMEM((TW, TW), BF16),
            pltpu.VMEM((2, TW, FB), BF16),
            pltpu.VMEM((FB, TW), BF16),
            pltpu.VMEM((TW, SW), BF16),
            pltpu.VMEM((ROWS, SW), BF16),
            pltpu.VMEM((4, SW, SW), BF16),
            pltpu.VMEM((6, ROWS, 128), F32),
            pltpu.VMEM((ROWS, SW), BF16),
            pltpu.VMEM((256, 384), BF16),
            pltpu.VMEM((64, 384), BF16),
            pltpu.VMEM((16, 384), BF16),
            pltpu.VMEM((768, TW), BF16),
            pltpu.VMEM((3, TW, TP), BF16),
            pltpu.VMEM((8, 8, TW), F32),
            pltpu.SemaphoreType.DMA((7,)),
            pltpu.SemaphoreType.DMA((1,)),
            pltpu.SemaphoreType.DMA((5,)),
            pltpu.SemaphoreType.DMA((10,)),
            pltpu.SemaphoreType.DMA((10,)),
            pltpu.SemaphoreType.DMA((3,)),
            pltpu.SemaphoreType.DMA((3,)),
        ],
        compiler_params=pltpu.CompilerParams(
            collective_id=0, has_side_effects=True, vmem_limit_bytes=60 * 1024 * 1024
        ),
        name="encode",
    )(patches, w_patch, w_tqkv, w_to, w_gu, w_down, w_in, tokens, w_slide, tgain, sgain)


def attend(q, keys, values):
    s = dot_nt(q, keys)
    m = jnp.max(s, axis=-1, keepdims=True)
    e = jnp.exp2((s - m) * (LOG2E * SH**-0.5)).astype(BF16)
    return e, dot(e, values)


def slide_kernel(
    info,
    qkv0,
    q1,
    q2,
    q3,
    kv1,
    kv2,
    kv3,
    tokens,
    new,
    em,
    w_so,
    out,
    qkv0_s,
    q1_s,
    q2_s,
    q3_s,
    kv1_s,
    kv2_s,
    kv3_s,
    tok_s,
    far_s,
    sem,
):
    step = pl.program_id(0)

    @pl.when(step == 0)
    def _():
        place = info[48]
        copies = [
            pltpu.make_async_copy(src, dst, sem.at[at])
            for at, (src, dst) in enumerate(
                (
                    (qkv0, qkv0_s),
                    (q1, q1_s),
                    (q2, q2_s),
                    (q3, q3_s),
                    (kv1, kv1_s),
                    (kv2, kv2_s),
                    (kv3, kv3_s),
                    (tokens, tok_s),
                )
            )
        ]
        for copy in copies:
            copy.start()
        far_s[...] = jnp.zeros_like(far_s)
        for copy in copies:
            copy.wait()

        def put(ref, row, vector, columns=None):
            base = pl.multiple_of((row // 16) * 16, 16)
            width = ref.shape[1]
            block = ref[pl.ds(base, 16), :].astype(F32)
            hit = lax.broadcasted_iota(jnp.int32, (16, width), 0) == row - base
            if columns is not None:
                hit = jnp.logical_and(hit, columns)
            ref[pl.ds(base, 16), :] = jnp.where(hit, vector, block).astype(BF16)

        head16 = head_of((16, 384))

        @pl.loop(0, 48)
        def _(n):
            pos = info[n]
            row = (n // 3) * 8 + n % 3
            local = pos // ROWS == place
            here = pos % ROWS

            @pl.when(local)
            def _():
                vector = new[pl.ds(row, 1), 0:SW]
                ones = lax.broadcasted_iota(jnp.int32, (1, SW), 1) == 2 * 256 + GW
                put(qkv0_s, here, jnp.where(ones, 1.0, vector))
                put(tok_s, here, em[pl.ds(row, 1), :])

            for p, q_s, kv_s in ((1, q1_s, kv1_s), (2, q2_s, kv2_s), (3, q3_s, kv3_s)):
                r = DIL[p]
                count = ROWS // r
                owner = pos // ROWS
                seen = pos % r < 4
                within = owner // r == place // r
                if p == 1:
                    slot = owner % 8
                else:
                    grp = owner // 8
                    at_chip = (grp // 2) * 8 + owner % 8
                    slot = (grp % 2) * 16 + at_chip % 16 if p == 2 else (grp % 2) * 64 + at_chip
                columns = head16 == pos % r

                @pl.when(jnp.logical_and(seen, within))
                def _():
                    put(
                        kv_s,
                        slot * count + here // r,
                        new[pl.ds(row, 1), p * SW : p * SW + 384],
                        columns,
                    )

                    @pl.when(local)
                    def _():
                        put(
                            q_s,
                            here // r,
                            new[pl.ds(row, 1), p * SW + 384 : (p + 1) * SW],
                            columns,
                        )

        for p, q_s, kv_s in ((1, q1_s, kv1_s), (2, q2_s, kv2_s), (3, q3_s, kv3_s)):
            r = DIL[p]
            count = ROWS // r
            q = q_s[...]
            kv = kv_s[...]
            head = head_of((count, 384))
            for j in range(4):
                e, o = attend(jnp.where(head == j, q, jnp.zeros_like(q)), kv, kv)
                total = jnp.sum(e.astype(F32), axis=-1, keepdims=True)
                lane = lax.broadcasted_iota(jnp.int32, (count, 256), 1)
                mine = jnp.logical_and(lane >= j * SH, lane < (j + 1) * SH)
                o = jnp.where(mine, o[:, 0:256] / total, 0.0)
                for b in range(2):
                    far_s[2 * (p - 1) + b, pl.ds(j, count, stride=r), :] = o[
                        :, b * 128 : (b + 1) * 128
                    ]

    at = pl.ds(pl.multiple_of(step * 256, 256), 256)
    q = qkv0_s[at, 0:256]
    k = qkv0_s[:, 256:512]
    v = qkv0_s[:, 512:768]
    lane = lax.broadcasted_iota(jnp.int32, (256, 256), 1)
    near = jnp.zeros((256, 256), F32)
    for j in range(4):
        mine = jnp.logical_and(lane >= j * SH, lane < (j + 1) * SH)
        _, o = attend(jnp.where(mine, q, jnp.zeros_like(q)), k, v)
        near = jnp.where(mine, o / o[:, GW : GW + 1], near)
    total = tok_s[at, :].astype(F32) + dot(near.astype(BF16), w_so[0:256, :])
    for p in range(3):
        far = jnp.concatenate([far_s[2 * p, at, :], far_s[2 * p + 1, at, :]], axis=1)
        total = total + dot(far.astype(BF16), w_so[(p + 1) * 256 : (p + 2) * 256, :])
    out[...] = total.astype(BF16)


def run_slide(info, qkv0, q1, q2, q3, kv1, kv2, kv3, tokens, new, em, w_so):
    hbm = pl.BlockSpec(memory_space=pl.ANY)

    def whole(a):
        return pl.BlockSpec(a.shape, lambda i, info: (0,) * a.ndim)

    return pl.pallas_call(
        slide_kernel,
        out_shape=jax.ShapeDtypeStruct((ROWS, SW), BF16),
        grid_spec=pltpu.PrefetchScalarGridSpec(
            num_scalar_prefetch=1,
            grid=(8,),
            in_specs=[hbm] * 8 + [whole(new), whole(em), whole(w_so)],
            out_specs=pl.BlockSpec((256, SW), lambda i, info: (i, 0)),
            scratch_shapes=[
                pltpu.VMEM((ROWS, SW), BF16),
                pltpu.VMEM((256, 384), BF16),
                pltpu.VMEM((64, 384), BF16),
                pltpu.VMEM((16, 384), BF16),
                pltpu.VMEM((2048, 384), BF16),
                pltpu.VMEM((2048, 384), BF16),
                pltpu.VMEM((2048, 384), BF16),
                pltpu.VMEM((ROWS, SW), BF16),
                pltpu.VMEM((6, ROWS, 128), F32),
                pltpu.SemaphoreType.DMA((8,)),
            ],
        ),
        compiler_params=pltpu.CompilerParams(vmem_limit_bytes=56 * 1024 * 1024),
        name="slide",
    )(info, qkv0, q1, q2, q3, kv1, kv2, kv3, tokens, new, em, w_so)


def shards(
    tile_patches,
    w_patch,
    w_tqkv,
    w_to,
    w_gu,
    w_down,
    tile_gain,
    w_in,
    slide_tokens,
    slide_gain,
    w_sqkv,
    w_so,
    pattern_of_group,
    new_positions,
):
    grp = lax.axis_index("grp")
    place = grp * 8 + lax.axis_index("dev")
    uses = [pattern_of_group == p for p in range(4)]

    def columns(index, p):
        part = w_sqkv[index, :, 3 * GW :]
        for g in range(3):
            part = jnp.where(uses[p][g], w_sqkv[index, :, g * GW : (g + 1) * GW], part)
        return part

    def rows(p):
        part = w_so[3 * GW :]
        for g in range(3):
            part = jnp.where(uses[p][g], w_so[g * GW : (g + 1) * GW], part)
        return part

    gap = jnp.zeros((SW, 64), BF16)
    wide = jnp.zeros((SW, GW), BF16)
    w_slide = [
        jnp.concatenate(
            [columns(0, 0), gap, columns(1, 0), gap, columns(2, 0), gap], axis=1
        )
    ] + [
        jnp.concatenate([columns(2, p), columns(1, p), wide, columns(0, p)], axis=1)
        for p in (1, 2, 3)
    ]
    w_slide = jnp.stack(w_slide)
    (
        qkv0,
        q1,
        q2,
        q3,
        kv1,
        kv2,
        kv3,
        em,
        new,
    ) = run_encoder(
        tile_patches,
        w_patch,
        w_tqkv,
        w_to,
        w_gu,
        w_down,
        w_in,
        slide_tokens,
        w_slide,
        tile_gain,
        slide_gain.reshape(1, SW),
    )
    pad = jnp.zeros((64, SW), BF16)
    w_out = jnp.concatenate(
        [piece for p in range(4) for piece in (rows(p), pad)], axis=0
    )
    info = jnp.concatenate([new_positions, place.astype(jnp.int32).reshape(1)])
    slide_out = run_slide(
        info, qkv0, q1, q2, q3, kv1, kv2, kv3, slide_tokens, new, em.reshape(128, SW), w_out
    )
    tile_embed = lax.dynamic_slice_in_dim(em, grp, 1, 0)[0, 0:3].astype(BF16)
    return (tile_embed, slide_out)


def solution(mesh):
    placed = (
        P(("grp", "dev"), None),
        P(),
        P(None, None, "dev"),
        P("dev", None),
        P(None, None, "dev"),
        P("dev", None),
        P(),
        P(),
        P(("grp", "dev"), None),
        P(),
        P(),
        P(),
        P(),
        P(),
    )
    return jax.shard_map(
        shards,
        mesh=mesh,
        in_specs=placed,
        out_specs=(P("grp", None), P(("grp", "dev"), None)),
        check_vma=False,
    )
```

time: 704 us -> 245 us (0.35); the launches traced: 694 us -> 243 us
  waiting for transfers between devices: 257 us -> 0 us
  Pallas kernels: 0 us -> 191 us
  local copies, waits for them, and re-layouts: 148 us -> 11.9 us
  blocking collectives: 129 us -> 0 us
  matrix products: 112 us -> 0 us
  other arithmetic: 12.5 us -> 39.4 us
  between operations: 18 us -> 0.78 us
  starting transfers between devices: 17.1 us -> 0 us
    all_gather x2 -> x0, waiting for transfers between devices: 237 us -> none  [side_by_side(): lax.all_gather(both, axis, axis=dim, tiled=True)]
    pallas_call x0 -> x2, Pallas kernels: none -> 191 us  [the longest x1 135 us: run_encoder(): pl.pallas_call(encoder_kernel, out_shape=(shape((ROWS, SW), BF16), shape(...]
    all_to_all x4 -> x0, blocking collectives: 129 us -> none  [the longest x2 68.4 us: from_everyone(): return lax.all_to_all(copies, axis, split_axis=0, concat_axis=0, tiled=True)]
    dot_general x20 -> x0, matrix products: 76.2 us -> none  [the longest x4 31.2 us: attend_segment(): jnp.einsum('hqk,khd->qhd', probs, values, preferred_element_type=jnp.floa...]
    dynamic_update_slice x4 -> x0, local copies, waits for them, and re-layouts: 42.6 us -> none  [shards(): lax.dynamic_update_slice(attended_slide, placed.reshape(row_count, width_...]
    sub x3 -> x0, matrix products: 35.8 us -> none  [attend_segment(): probs = jax.nn.softmax(scores, axis=-1).astype(jnp.bfloat16)]
    select_n x0 -> x5, other arithmetic: none -> 24 us  [columns(): part = jnp.where(uses[p][g], w_sqkv[index, :, g * GW:(g + 1) * GW], part)]
    reshape x14 -> x1, local copies, waits for them, and re-layouts: 22.3 us -> 0.58 us  [shards(): slide_gain.reshape(1, SW)]
  transfers between devices with their start and end apart: 4 -> 0, of which waited for: 3 -> 0; matrix products, arithmetic and copies ran while one was open for 18% -> 0% of each run, Pallas kernels for 0% -> 0%
where the time goes in v1:
time: 245 us; the launch traced here: 243 us
  Pallas kernels  191 us (78%)
  other arithmetic  39.4 us (16%)
  local copies, waits for them, and re-layouts  11.9 us (5%)
    pallas_call x1, Pallas kernels, run_encoder(): pl.pallas_call(encoder_kernel, out_shape=(shape((ROWS, SW), BF16), shape(...  135 us
    pallas_call x1, Pallas kernels, run_slide(): pl.pallas_call(slide_kernel, out_shape=jax.ShapeDtypeStruct((ROWS, SW), B...  56.1 us
    select_n x5, other arithmetic, columns(): part = jnp.where(uses[p][g], w_sqkv[index, :, g * GW:(g + 1) * GW], part)  24 us
    unnamed x4, other arithmetic  8.14 us
    another operation x2, other arithmetic, shards(): w_slide = jnp.stack(w_slide)  5.83 us

profile of v1, /device:TPU:1, one launch (start us, length us, event | category | flops | bytes accessed | tf_op | source)
XLA Modules:
  0.0 242.9 jit_solution(4361561864352066306)
XLA Ops:
  0.6 0.7 broadcast_compare_fusion.3
  1.3 0.6 fusion.1
  1.9 0.7 fusion.3
  2.6 7.4 %select_bitcast_fusion.9 = (bf16[768,192]{1,0:T(8,128)(2,1)}, bf16[768,192]{1,0:T(8,128)(2,1)S(1)}, bf16[768,192]{1,0:T(8,128)(2,1)S(1)}) fusion(pred[]{:T(512)} %bitcast.2, pred[]{:T(512)} %bitcast.1, pred[]{:T(512)} %bitcast, bf16[3,768,768]{2,1,0:T(8,128)(2,1)} %param.24, pred[]{:T(512)} %bitcast.16, pred[]{:T(512)} %bitcast.15, pred[]{:T(512)} %bitcast.14), kind=kLoop, calls=%fused_computation.13 | loop fusion | flops 1327104 | bytes 3244038 | tf_op jit(solution)/shard_map/jit(_where)/select_n | solution.py:608
  10.0 5.0 %select_bitcast_fusion.10 = (bf16[768,192]{1,0:T(8,128)(2,1)}, bf16[768,192]{1,0:T(8,128)(2,1)S(1)}, bf16[768,192]{1,0:T(8,128)(2,1)S(1)}) fusion(pred[]{:T(512)} %bitcast.2, pred[]{:T(512)} %bitcast.1, pred[]{:T(512)} %bitcast, bf16[3,768,768]{2,1,0:T(8,128)(2,1)S(1)} %copy-done, pred[]{:T(512)} %bitcast.23, pred[]{:T(512)} %bitcast.22, pred[]{:T(512)} %bitcast.21), kind=kLoop, calls=%fused_computation.14 | loop fusion | flops 1327104 | bytes 3244038 | tf_op jit(solution)/shard_map/jit(_where)/select_n | solution.py:608
  15.1 4.9 %select_bitcast_fusion.11 = (bf16[768,192]{1,0:T(8,128)(2,1)}, bf16[768,192]{1,0:T(8,128)(2,1)S(1)}, bf16[768,192]{1,0:T(8,128)(2,1)S(1)}) fusion(pred[]{:T(512)} %bitcast.2, pred[]{:T(512)} %bitcast.1, pred[]{:T(512)} %bitcast, bf16[3,768,768]{2,1,0:T(8,128)(2,1)S(1)} %copy-done, pred[]{:T(512)} %bitcast.9, pred[]{:T(512)} %bitcast.8, pred[]{:T(512)} %bitcast.7), kind=kLoop, calls=%fused_computation.15 | loop fusion | flops 1327104 | bytes 3244038 | tf_op jit(solution)/shard_map/jit(_where)/select_n | solution.py:608
  20.0 4.4 %select_bitcast_fusion.8 = (bf16[768,192]{1,0:T(8,128)(2,1)S(1)}, bf16[768,192]{1,0:T(8,128)(2,1)S(1)}) fusion(pred[]{:T(512)} %bitcast.9, pred[]{:T(512)} %bitcast.8, pred[]{:T(512)} %bitcast.7, bf16[3,768,768]{2,1,0:T(8,128)(2,1)S(1)} %copy-done, pred[]{:T(512)} %bitcast.16, pred[]{:T(512)} %bitcast.15, pred[]{:T(512)} %bitcast.14), kind=kLoop, calls=%fused_computation.12 | loop fusion | flops 884736 | bytes 2949126 | tf_op jit(solution)/shard_map/jit(_where)/select_n | solution.py:608
  24.4 2.2 select_bitcast_fusion
  26.6 2.3 maximum_bitcast_fusion
  29.0 0.7 broadcast_in_dim.9
  29.7 3.6 %concatenate.18 = bf16[768,768]{1,0:T(8,128)(2,1)} concatenate(bf16[768,192]{1,0:T(8,128)(2,1)} %get-tuple-element.26, bf16[768,64]{1,0:T(8,128)(2,1)} %broadcast_in_dim.9, bf16[768,192]{1,0:T(8,128)(2,1)} %get-tuple-element.23, bf16[768,64]{1,0:T(8,128)(2,1)} %broadcast_in_dim.9, bf16[768,192]{1,0:T(8,128)(2,1)} %get-tuple-element.20, bf16[768,64]{1,0:T(8,128)(2,1)} %broadcast_in_dim.9), dimensions={1} | concatenate | bytes 2359296 | tf_op jit(solution)/shard_map/concatenate | solution.py:620
  33.3 3.5 %pad_maximum_fusion.w_slide = bf16[4,768,768]{2,1,0:T(8,128)(2,1)} fusion(bf16[1,768,768]{2,1,0:T(8,128)(2,1)S(1)} %get-tuple-element.33, bf16[1,768,768]{2,1,0:T(8,128)(2,1)S(1)} %get-tuple-element.32, bf16[1,768,768]{2,1,0:T(8,128)(2,1)S(1)} %get-tuple-element.31, bf16[1,768,768]{2,1,0:T(8,128)(2,1)} %bitcast.47), kind=kLoop, calls=%fused_computation | loop fusion | flops 7077888 | bytes 9437184 | tf_op jit(solution)/shard_map/stack | solution.py:627
  36.8 4.0 %copy.16.w_tqkv = bf16[3,1536,192]{2,1,0:T(8,128)(2,1)} copy(bf16[3,1536,192]{1,2,0:T(8,128)(2,1)} %param.16) | data formatting | bytes 3538944 | tf_op args[2]
  40.7 0.6 reshape.86.sgain
  41.3 134.7 %encode.1 = (bf16[2048,768]{1,0:T(8,128)(2,1)}, bf16[256,384]{1,0:T(8,128)(2,1)}, bf16[64,384]{1,0:T(8,128)(2,1)}, bf16[16,384]{1,0:T(8,128)(2,1)}, bf16[2048,38...) custom-call(bf16[96,588]{1,0:T(8,128)(2,1)} %patches.1, ...), custom_call_target="tpu_custom_call" | custom-call | tf_op jit(solution)/shard_map/encode/pallas_call | solution.py:356
  176.1 2.0 select_dynamic-update-slice_fusion.3
  178.1 2.0 select_dynamic-update-slice_fusion.2
  180.0 0.0 copy-start.4
  180.1 2.2 select_dynamic-update-slice_fusion.1
  182.2 2.1 select_dynamic-update-slice_fusion
  184.3 0.8 pad_add_fusion.info
  185.1 0.4 copy-done.2
  185.5 56.1 %slide.1 = bf16[2048,768]{1,0:T(8,128)(2,1)} custom-call(s32[49]{0:T(128)} %pad_add_fusion.info, bf16[2048,768]{1,0:T(8,128)(2,1)} %get-tuple-element.12.qkv0, bf16[256,384]{1,0:T(8,128)(2,1)} %get-tuple-element.13.q1, bf16[64,384]{1,0:T(8,128)(2,1)} %get-tuple-element.14.q2, bf16[16,384]{1,0:T(8,128)(2,1)} %get-tuple-element.15.q3, ...), custom_call_target="tpu_custom_call" | custom-call | tf_op jit(solution)/shard_map/slide/pallas_call | solution.py:559
  241.6 1.3 fusion
  (14 shorter events, 0.1 us)
Async XLA Ops:
  2.6 7.4 %copy-start = (bf16[3,768,768]{2,1,0:T(8,128)(2,1)S(1)}, bf16[3,768,768]{2,1,0:T(8,128)(2,1)}, u32[]{:S(2)}) copy-start(bf16[3,768,768]{2,1,0:T(8,128)(2,1)} %param.24) | copy-start | bytes 10616836
  36.8 4.0 %copy-start.3 = (f32[768]{0:T(1024)S(1)}, f32[768]{0:T(1024)}, u32[]{:S(2)}) copy-start(f32[768]{0:T(1024)} %param.23) | copy-start | bytes 9220
  41.3 134.8 %copy-start.1 = (bf16[768,768]{1,0:T(8,128)(2,1)S(1)}, bf16[768,768]{1,0:T(8,128)(2,1)}, u32[]{:S(2)}) copy-start(bf16[768,768]{1,0:T(8,128)(2,1)} %param.25) | copy-start | bytes 3538948
  180.0 4.3 %copy-start.4 = (s32[48]{0:T(128)S(1)}, s32[48]{0:T(128)}, u32[]{:S(2)}) copy-start(s32[48]{0:T(128)} %param.27) | copy-start | bytes 580
  184.3 1.2 copy-start.2
